TPU v7x, 256 devices: a whole 4x4x8 slice. The times are simulated.
256 devices in a mesh: row: 16 (over x, y), col: 16 (over z, core).
Axes of the slice: x: 4, y: 4, z: 8, core: 2. Of those that a mesh axis runs over, the one named last changes fastest.
Arguments:
- panel: float32 [131072, 256], P(('row', 'col')), may hold values from -1 to 1
- image_rest: float32 [131072, 256], P(('row', 'col')), may hold values from -300 to 300
- a_slab: float32 [131072, 2048], P('row', 'col'), may hold values from -288 to 288
Outputs:
- r_factor: float32 [256, 256], replicated
- slab_update: float32 [131072, 2048], P('row', 'col')
All inputs are finite; a program needn't handle non-finite values.
Results may differ from a plain program's by a relative error of at most 0.000082.
Values sent between devices are 32-bit elements; how exact they have to be, the bound alone decides.
A program may use at most 128 MiB of HBM per device.

v0:
```python
import jax
import jax.numpy as jnp
from jax import lax
from jax.sharding import PartitionSpec as P


def contract_first(left, right):
    return lax.dot_general(
        left,
        right,
        (((0,), (0,)), ((), ())),
        precision=lax.Precision.HIGHEST,
        preferred_element_type=jnp.float32,
    )


def contract_last(left, right):
    return lax.dot_general(
        left,
        right,
        (((1,), (1,)), ((), ())),
        precision=lax.Precision.HIGHEST,
        preferred_element_type=jnp.float32,
    )


def per_device(panel, image_rest, a_slab):
    highest = lax.Precision.HIGHEST
    row_count = lax.axis_size("row")
    slab_local = a_slab.shape[1]
    slab_rows = slab_local // row_count
    gram_matrix = lax.psum(contract_first(panel, panel), ("row", "col"))
    lower_factor = jnp.linalg.cholesky(gram_matrix)
    r_factor = lower_factor.T
    basis_rows = lax.linalg.triangular_solve(
        lower_factor, panel, left_side=False, lower=True, transpose_a=True
    )
    basis_slab = lax.all_gather(basis_rows[:slab_rows], "row", axis=0, tiled=True)
    image_full = image_rest + lax.psum_scatter(
        2.0 * jnp.dot(a_slab, basis_slab, precision=highest, preferred_element_type=jnp.float32),
        "col",
        scatter_dimension=0,
        tiled=True,
    )
    coupling = lax.psum(contract_first(basis_rows, image_full), ("row", "col"))
    reduced = image_full - jnp.dot(
        basis_rows, coupling, precision=highest, preferred_element_type=jnp.float32
    )
    paired = jnp.concatenate([basis_rows, reduced], axis=1)
    reduced_slab = lax.all_gather(reduced[:slab_rows], "row", axis=0, tiled=True)
    partner = jnp.concatenate([reduced_slab, basis_slab], axis=1)
    slab_update = contract_last(lax.all_gather(paired, "col", axis=0, tiled=True), partner)
    return (r_factor, slab_update)


def solution(mesh):
    placed = (P(("row", "col"), None), P(("row", "col"), None), P("row", "col"))
    return jax.shard_map(
        per_device, mesh=mesh, in_specs=placed, out_specs=(P(), P("row", "col")), check_vma=False
    )
```

profile of v0, /device:TPU:1, one launch (start us, length us, event | category | flops | bytes accessed | tf_op | source)
XLA Modules:
  0.0 824.0 jit_solution(1246861324995275793)
XLA Ops:
  7.2 2.9 fusion.20
  10.2 256.4 %all-reduce.4.cloned.1.call-done = f32[256,256]{0,1:T(8,128)} async-done(((f32[256,256]{0,1:T(8,128)}), f32[256,256]{0,1:T(8,128)}) %all-reduce.4.cloned.1.call-update) | async-done | bytes 262160 | tf_op jit(solution)/shard_map/psum | solution.py:32
  266.6 1.1 copy.11
  267.7 1.0 fusion.6
  268.7 11.7 %cholesky.50 = f32[128,128]{1,0:T(8,128)S(1)} custom-call(f32[128,128]{1,0:T(8,128)S(1)} %cholesky.118), custom_call_target="Cholesky" | custom-call | tf_op jit(solution)/shard_map/jit(cholesky)/cholesky | solution.py:33
  280.5 9.8 %custom-call.14 = f32[1,128,128]{1,2,0:T(8,128)S(1)} custom-call(f32[1,128,128]{2,1,0:T(8,128)S(1)} %get-tuple-element.29), custom_call_target="InvertDiagBlocksLowerTriangular" | custom-call | tf_op jit(solution)/shard_map/jit(cholesky)/cholesky | solution.py:33
  290.8 11.7 %cholesky.105 = f32[128,128]{1,0:T(8,128)S(1)} custom-call(f32[128,128]{1,0:T(8,128)S(1)} %convolution_subtract_fusion.2), custom_call_target="Cholesky" | custom-call | tf_op jit(solution)/shard_map/jit(cholesky)/cholesky | solution.py:33
  304.6 4.1 while.1
  305.3 1.4 bitcast_dynamic-update-slice_fusion.2
  307.3 1.4 bitcast_dynamic-update-slice_fusion.2
  308.7 19.7 %custom-call.15 = f32[2,128,128]{1,2,0:T(8,128)S(1)} custom-call(f32[2,128,128]{2,1,0:T(8,128)S(1)} %get-tuple-element.9), custom_call_target="InvertDiagBlocksLowerTriangular" | custom-call | tf_op jit(solution)/shard_map/triangular_solve | solution.py:35
  328.4 1.4 fusion.7
  329.8 1.5 convolution_subtract_fusion.1
  331.9 18.0 %all_gather.9 = f32[128,256]{1,0:T(8,128)S(1)} all-gather(f32[8,256]{1,0:T(8,128)S(1)} %copy.12), channel_id=1, replica_groups=mesh['row'=16,'col'=16] {'row'}, dimensions={0}, use_global_device_ids=true | all-gather | bytes 139264 | tf_op jit(solution)/shard_map/all_gather | solution.py:38
  349.8 10.8 %fusion = f32[8192,256]{0,1:T(8,128)} fusion(f32[128,256]{1,0:T(8,128)S(1)} %all_gather.9, f32[8192,128]{1,0:T(8,128)} %param.5), kind=kOutput, calls=%fused_computation.3 | convolution fusion | flops 3223322624 | bytes 12713984 | tf_op jit(solution)/shard_map/dot_general | solution.py:40
  360.9 71.5 %reduce-scatter.2.cloned.1.call-done = f32[512,256]{0,1:T(8,128)} async-done(((f32[8192,256]{0,1:T(8,128)}), f32[512,256]{0,1:T(8,128)}) %reduce-scatter.2.cloned.1.call-update) | async-done | bytes 524304 | tf_op jit(solution)/shard_map/reduce_scatter | solution.py:39
  432.4 1.1 add.32
  433.5 1.3 fusion.1
  434.9 254.0 %all-reduce.6.cloned.1.call-done = f32[256,256]{1,0:T(8,128)} async-done(((f32[256,256]{1,0:T(8,128)}), f32[256,256]{1,0:T(8,128)}) %all-reduce.6.cloned.1.call-update) | async-done | bytes 262160 | tf_op jit(solution)/shard_map/psum | solution.py:45
  688.9 1.6 convolution_subtract_fusion
  690.5 1.0 pad_maximum_fusion
  692.5 18.8 %all_gather.11 = f32[128,256]{1,0:T(8,128)S(1)} all-gather(f32[8,256]{1,0:T(8,128)S(1)} %copy.15), channel_id=1, replica_groups=mesh['row'=16,'col'=16] {'row'}, dimensions={0}, use_global_device_ids=true | all-gather | bytes 139264 | tf_op jit(solution)/shard_map/all_gather | solution.py:50
  711.2 76.3 %all-gather.2.cloned.1.call-done = f32[8192,512]{0,1:T(8,128)} async-done(((f32[512,512]{0,1:T(8,128)}), f32[8192,512]{0,1:T(8,128)}) %all-gather.2.cloned.1.call-update) | async-done | bytes 16777232 | tf_op jit(solution)/shard_map/all_gather | solution.py:52
  787.6 29.9 %fusion.2 = f32[8192,128]{1,0:T(8,128)} fusion(f32[8192,512]{0,1:T(8,128)} %all-gather.2.cloned.1.call-done, f32[128,256]{1,0:T(8,128)S(1)} %all_gather.9, f32[128,256]{1,0:T(8,128)S(1)} %all_gather.11), kind=kOutput, calls=%fused_computation.10 | convolution fusion | flops 6442516480 | bytes 21233664 | tf_op jit(solution)/shard_map/dot_general | solution.py:18
  (32 shorter events, 4.3 us)
Async XLA Ops:
  7.2 259.5 %all-reduce.4.cloned.1.call-start = ((), (), s32[]{:S(2)}) async-start(), calls=%async_computation.1 | async-start | bytes 524288 | tf_op jit(solution)/shard_map/psum | solution.py:32
  10.1 422.3 %reduce-scatter.2.cloned.1.call-start = ((), (), s32[]{:S(2)}) async-start(), calls=%async_computation.2 | async-start | bytes 8912896 | tf_op jit(solution)/shard_map/reduce_scatter | solution.py:39
  349.8 10.9 %copy-start = (f32[512,256]{1,0:T(8,128)S(1)}, f32[512,256]{1,0:T(8,128)}, u32[]{:S(2)}) copy-start(f32[512,256]{1,0:T(8,128)} %param.4) | copy-start | bytes 1572868
  360.7 328.2 %all-reduce.6.cloned.1.call-start = ((), (), s32[]{:S(2)}) async-start(), calls=%async_computation.3 | async-start | bytes 524288 | tf_op jit(solution)/shard_map/psum | solution.py:45
  434.9 352.7 %all-gather.2.cloned.1.call-start = ((), (), s32[]{:S(2)}) async-start(), calls=%async_computation.4 | async-start | bytes 17825792 | tf_op jit(solution)/shard_map/all_gather | solution.py:52
Sparse Core Ops, SparseCore 0:
  14.0 252.5 all-reduce.3
  360.8 71.5 reduce-scatter.1
  438.4 250.3 all-reduce.5
  691.7 95.8 all-gather.1
where the time goes:
time: 824 us
  waiting for transfers between devices  658 us (80%)
  other arithmetic  56.8 us (7%)
  matrix products  50.4 us (6%)
  blocking collectives  36.7 us (4%)
  between operations  15.2 us (2%)
    psum x1, waiting for transfers between devices, per_device(): gram_matrix = lax.psum(contract_first(panel, panel), ('row', 'col'))  256 us
    psum x1, waiting for transfers between devices, per_device(): coupling = lax.psum(contract_first(basis_rows, image_full), ('row', 'col'))  254 us
    all_gather x1, waiting for transfers between devices, per_device(): lax.all_gather(paired, 'col', axis=0, tiled=True)  76.3 us
    reduce_scatter x1, waiting for transfers between devices, per_device(): lax.psum_scatter(2.0 * jnp.dot(a_slab, basis_slab, precision=highest, pre...  71.5 us
    another operation x6, other arithmetic, per_device(): lower_factor = jnp.linalg.cholesky(gram_matrix)  34 us
    dot_general x1, matrix products, contract_last(): lax.dot_general(left, right, (((1,), (1,)), ((), ())), precision=lax.Prec...  29.9 us
    another operation x3, other arithmetic, per_device(): lax.linalg.triangular_solve(lower_factor, panel, left_side=False, lower=T...  19.7 us
    all_gather x1, blocking collectives, per_device(): lax.all_gather(reduced[:slab_rows], 'row', axis=0, tiled=True)  18.8 us
  transfers between devices with their start and end apart: 4, of which 4 were waited for; matrix products, arithmetic and copies ran while one was open for 0% of the time, Pallas kernels for 0%

commit v1 on v0

v1 whole, which is shorter than its diff:
```python
import functools

import jax
import jax.numpy as jnp
from jax import lax
from jax.experimental import pallas as pl
from jax.experimental.pallas import tpu as pltpu
from jax.sharding import PartitionSpec as P

MESH = pl.DeviceIdType.MESH
HIGHEST = lax.Precision.HIGHEST
PIECE = 8


def dot(left, right, contract=((1,), (0,))):
    return lax.dot_general(
        left, right, (contract, ((), ())), precision=HIGHEST, preferred_element_type=jnp.float32
    )


def kernel(
    rows,
    chips,
    panel_hbm,
    rest_hbm,
    a_hbm,
    r_ref,
    out_hbm,
    a_buf,
    p_all,
    z_all,
    t_part,
    t_recv,
    rest,
    p_slab,
    z_slab,
    gram_src,
    gram_recv,
    gram_line,
    gram,
    coup_src,
    coup_recv,
    coup_line,
    coup,
    work,
    lower_inv,
    basis_slab_t,
    mix,
    staged,
    local_sem,
    a_local_sem,
    a_send_sem,
    a_recv_sem,
    plane_send_sem,
    plane_recv_sem,
    line_send_sem,
    line_recv_sem,
    ring_send_sem,
    ring_recv_sem,
    out_local_sem,
    out_send_sem,
    out_recv_sem,
):
    r = lax.axis_index("row")
    c = lax.axis_index("col")
    z = c // 2
    core = c % 2
    plane = 2 * rows
    q = core * rows + r
    half_ring = chips // 2
    half = p_all.shape[2]
    block = 2 * half
    width = p_all.shape[3]
    steps = chips - 1

    def chip(offset):
        return (z + offset + 2 * chips) % chips

    def at_plane(index):
        return (index % rows, 2 * z + index // rows)

    def at_chip(index):
        return (r, 2 * index + core)

    right, left = at_chip(chip(1)), at_chip(chip(-1))
    sibling = (r, 2 * z + (1 - core))

    panel_load = [
        pltpu.make_async_copy(
            panel_hbm.at[pl.ds(h * half, half)], p_all.at[z, h], local_sem.at[h]
        )
        for h in range(2)
    ]
    rest_load = [
        pltpu.make_async_copy(
            rest_hbm.at[pl.ds(h * half, half)], rest.at[h], local_sem.at[2 + h]
        )
        for h in range(2)
    ]

    def block_of(i):
        magnitude = half_ring - (i + 1) // 2
        sign = 1 - 2 * ((i + 1) % 2)
        return chip(jnp.where(i == 0, half_ring, magnitude * sign))

    def a_local(i):
        target = block_of(i)
        start = pl.multiple_of((2 * target + core) * block, block)
        return pltpu.make_async_copy(
            a_hbm.at[pl.ds(start, block)], a_buf.at[core, target], a_local_sem.at[i]
        )

    def a_remote(i):
        target = block_of(i)
        start = pl.multiple_of((2 * target + 1 - core) * block, block)
        return pltpu.make_async_remote_copy(
            src_ref=a_hbm.at[pl.ds(start, block)],
            dst_ref=a_buf.at[core, target],
            send_sem=a_send_sem.at[i],
            recv_sem=a_recv_sem.at[i],
            device_id=sibling,
            device_id_type=MESH,
        )

    for copy in panel_load + rest_load:
        copy.start()

    @pl.loop(0, chips)
    def _(i):
        a_local(i).start()

    barrier = pltpu.get_barrier_semaphore()

    @pl.loop(1, plane)
    def _(i):
        pl.semaphore_signal(
            barrier, inc=1, device_id=at_plane((q + i) % plane), device_id_type=MESH
        )

    @pl.loop(1, chips)
    def _(i):
        pl.semaphore_signal(barrier, inc=1, device_id=at_chip(chip(i)), device_id_type=MESH)

    pl.semaphore_wait(barrier, plane - 1 + chips - 1)

    def plane_copy(i, src, dst, slot):
        return pltpu.make_async_remote_copy(
            src_ref=src,
            dst_ref=dst,
            send_sem=plane_send_sem.at[slot],
            recv_sem=plane_recv_sem.at[slot],
            device_id=at_plane((q + i) % plane),
            device_id_type=MESH,
        )

    def plane_gather_start(src, dst, slot):
        @pl.loop(1, plane)
        def _(i):
            plane_copy(i, src, dst.at[q], slot).start()

    def plane_scatter_start(src, dst, slot):
        @pl.loop(1, plane)
        def _(i):
            plane_copy(i, src.at[(q + i) % plane], dst.at[q], slot).start()

    def plane_wait_recv(dst, slot):
        whole = dst.at[pl.ds(0, plane - 1)]
        pltpu.make_async_copy(whole, whole, plane_recv_sem.at[slot]).wait()

    def plane_wait_send(dst, slot):
        whole = dst.at[pl.ds(0, plane - 1)]
        pltpu.make_async_copy(whole, whole, plane_send_sem.at[slot]).wait()

    def line_start(buf, slot):
        @pl.loop(1, chips)
        def _(i):
            pltpu.make_async_remote_copy(
                src_ref=buf.at[z],
                dst_ref=buf.at[z],
                send_sem=line_send_sem.at[slot],
                recv_sem=line_recv_sem.at[slot],
                device_id=at_chip(chip(i)),
                device_id_type=MESH,
            ).start()

    def line_wait(buf, sem, slot):
        whole = buf.at[pl.ds(0, chips - 1)]
        pltpu.make_async_copy(whole, whole, sem.at[slot]).wait()

    def sum_first(ref, count):
        total = ref[0]
        for i in range(1, count):
            total = total + ref[i]
        return total

    def ring(kind, direction, n, src, dst):
        return pltpu.make_async_remote_copy(
            src_ref=src,
            dst_ref=dst,
            send_sem=ring_send_sem.at[kind, direction, n],
            recv_sem=ring_recv_sem.at[kind, direction, n],
            device_id=(right, left)[direction],
            device_id_type=MESH,
        )

    def gather_slot(direction, n, shift):
        away = n // 2 + shift
        h = (1 if n % 2 == 0 else 0) if direction == 0 else (0 if n % 2 == 0 else 1)
        return chip(-away if direction == 0 else away), h

    def gather_copy(buf, kind, direction, n):
        at, h = gather_slot(direction, n, 0)
        return ring(kind, direction, n, buf.at[at, h], buf.at[at, h])

    def gather_wait(buf, kind, direction, n):
        at, h = gather_slot(direction, n, 1)
        ring(kind, direction, n, buf.at[at, h], buf.at[at, h]).wait_recv()

    waited = set()

    def gather_need(buf, kind, direction, n):
        if (kind, direction, n) not in waited:
            waited.add((kind, direction, n))
            gather_wait(buf, kind, direction, n)

    def gather_send(buf, kind, n):
        if n >= steps:
            return
        for direction in range(2):
            if n >= 2:
                gather_need(buf, kind, direction, n - 2)
            gather_copy(buf, kind, direction, n).start()

    def sum_slot(direction, n):
        away = half_ring - (n + 1) // 2
        h = n % 2 if direction == 0 else 1 - n % 2
        return chip(away if direction == 0 else -away), h

    def sum_copy(direction, n):
        at, h = sum_slot(direction, n)
        return ring(1, direction, n, t_part.at[at, h], t_recv.at[direction, n])

    def sum_send(n):
        if n >= steps:
            return
        for direction in range(2):
            if n >= 2:
                sum_copy(direction, n - 2).wait_recv()
                at, h = sum_slot(direction, n)
                t_part[at, h] = t_part[at, h] + t_recv[direction, n - 2]
            sum_copy(direction, n).start()

    def panel_send(n):
        gather_send(p_all, 0, n)

    def image_send(n):
        gather_send(z_all, 2, n)

    for copy in panel_load:
        copy.wait()
    plane_gather_start(p_all.at[z, 0, pl.ds(0, PIECE)], p_slab, 0)

    @pl.loop(0, chips)
    def _(i):
        a_remote(i).start()

    panel_send(0)
    panel_send(1)
    p_slab[q] = p_all[z, 0, 0:PIECE]
    own = p_all[z].reshape(block, width)
    gram_src[...] = dot(own, own, ((0,), (0,))).reshape(gram_src.shape)
    plane_scatter_start(gram_src, gram_recv, 1)
    gram_recv[q] = gram_src[q]

    def partial_sums(i):
        target = block_of(i)
        a_local(i).wait()
        pltpu.make_async_remote_copy(
            src_ref=a_buf.at[1 - core, target],
            dst_ref=a_buf.at[1 - core, target],
            send_sem=a_send_sem.at[i],
            recv_sem=a_recv_sem.at[i],
            device_id=sibling,
            device_id_type=MESH,
        ).wait_recv()
        slab = p_slab[...].reshape(plane * PIECE, width)
        both = jnp.concatenate([a_buf[0, target], a_buf[1, target]], axis=1)
        t_part[target] = dot(both, slab).reshape(2, half, width)

    plane_wait_recv(p_slab, 0)
    partial_sums(0)
    sum_send(0)

    @pl.loop(1, 3)
    def _(i):
        partial_sums(i)

    sum_send(1)

    @pl.loop(3, chips)
    def _(i):
        partial_sums(i)

    plane_wait_recv(gram_recv, 1)
    gram_line[z] = sum_first(gram_recv, plane)
    line_start(gram_line, 0)
    panel_send(2)
    line_wait(gram_line, line_recv_sem, 0)
    gram[q] = sum_first(gram_line, chips)
    plane_gather_start(gram.at[q], gram, 2)

    nb = width // 2
    chunk = nb // 4

    def eliminate(first):
        size = nb - first
        lanes = lax.broadcasted_iota(jnp.int32, (1, nb), 1)
        sub = lax.broadcasted_iota(jnp.int32, (size, 1), 0) + first

        @pl.loop(first, first + chunk)
        def _(j):
            pivot_row = work[pl.ds(j, 1), :]
            pick = lanes == j
            pivot = jnp.sum(jnp.where(pick, pivot_row[:, :nb], 0.0), axis=1, keepdims=True)
            body = work[first:, :]
            column = jnp.sum(jnp.where(pick, body[:, :nb], 0.0), axis=1, keepdims=True)
            factor = jnp.where(sub > j, column / pivot, 0.0)
            work[first:, :] = body - factor * pivot_row

    def load_work(matrix):
        row_id = lax.broadcasted_iota(jnp.int32, (nb, nb), 0)
        col_id = lax.broadcasted_iota(jnp.int32, (nb, nb), 1)
        work[:, :nb] = matrix
        work[:, nb:] = jnp.where(row_id == col_id, 1.0, 0.0)

    def factors():
        row_id = lax.broadcasted_iota(jnp.int32, (nb, nb), 0)
        col_id = lax.broadcasted_iota(jnp.int32, (nb, nb), 1)
        upper = work[:, :nb]
        diagonal = jnp.sum(jnp.where(row_id == col_id, upper, 0.0), axis=1, keepdims=True)
        scale = 1.0 / jnp.sqrt(diagonal)
        return jnp.where(col_id >= row_id, upper * scale, 0.0), work[:, nb:] * scale

    sum_send(2)
    plane_wait_recv(gram, 2)
    gram_rows = gram_src.shape[1]
    whole_gram = gram[...].reshape(plane * gram_rows, width)
    load_work(whole_gram[:nb, :nb])
    eliminate(0)
    sum_send(3)
    eliminate(chunk)
    panel_send(3)
    eliminate(2 * chunk)
    sum_send(4)
    eliminate(3 * chunk)
    upper_a, inverse_a = factors()
    r_ref[:nb, :nb] = upper_a
    lower_inv[:nb, :nb] = inverse_a
    whole_gram = gram[...].reshape(plane * gram_rows, width)
    cross = dot(inverse_a, whole_gram[:nb, nb:])
    r_ref[:nb, nb:] = cross
    r_ref[nb:, :nb] = jnp.zeros((nb, nb), jnp.float32)
    lower_inv[:nb, nb:] = jnp.zeros((nb, nb), jnp.float32)
    load_work(whole_gram[nb:, nb:] - dot(cross, cross, ((0,), (0,))))
    sum_send(5)
    eliminate(0)
    panel_send(4)
    eliminate(chunk)
    sum_send(6)
    eliminate(2 * chunk)
    panel_send(5)
    eliminate(3 * chunk)
    upper_b, inverse_b = factors()
    r_ref[nb:, nb:] = upper_b
    lower_inv[nb:, nb:] = inverse_b
    lower_inv[nb:, :nb] = -dot(inverse_b, dot(r_ref[:nb, nb:], lower_inv[:nb, :nb], ((0,), (0,))))

    inverse = lower_inv[...]
    basis_slab_t[...] = dot(
        inverse, p_slab[...].reshape(plane * PIECE, width), ((1,), (1,))
    )
    own_basis = dot(p_all[z].reshape(block, width), inverse, ((1,), (1,)))

    for copy in rest_load:
        copy.wait()
    for direction in range(2):
        for n in (steps - 2, steps - 1):
            sum_copy(direction, n).wait_recv()
    for h in range(2):
        first = t_recv[0, steps - 2 if h == 1 else steps - 1]
        second = t_recv[1, steps - 2 if h == 0 else steps - 1]
        total = t_part[z, h] + first + second
        z_all[z, h] = rest[h] + 2.0 * dot(total, inverse, ((1,), (1,)))
    image_send(0)
    image_send(1)
    plane_gather_start(z_all.at[z, 0, pl.ds(0, PIECE)], z_slab, 3)
    z_slab[q] = z_all[z, 0, 0:PIECE]
    coup_src[...] = dot(
        own_basis, z_all[z].reshape(block, width), ((0,), (0,))
    ).reshape(coup_src.shape)
    plane_scatter_start(coup_src, coup_recv, 4)
    coup_recv[q] = coup_src[q]
    panel_send(6)
    plane_wait_recv(coup_recv, 4)
    coup_line[z] = sum_first(coup_recv, plane)
    line_start(coup_line, 1)
    image_send(2)
    line_wait(coup_line, line_recv_sem, 1)
    coup[q] = sum_first(coup_line, chips)
    plane_gather_start(coup.at[q], coup, 5)
    image_send(3)
    plane_wait_recv(z_slab, 3)
    plane_wait_recv(coup, 5)
    coupling = coup[...].reshape(width, width)
    slab_t = basis_slab_t[...]
    inner = jnp.transpose(z_slab[...].reshape(plane * PIECE, width))
    inner = inner - dot(coupling, slab_t) - dot(coupling, slab_t, ((0,), (0,)))
    mix[...] = dot(lower_inv[...], inner, ((0,), (0,)))

    columns = plane * PIECE // 2

    def out_copies(slot, at, h):
        start = pl.multiple_of((2 * at + core) * block + h * half, half)
        local = pltpu.make_async_copy(
            staged.at[slot, core], out_hbm.at[pl.ds(start, half)], out_local_sem.at[slot]
        )
        remote = pltpu.make_async_remote_copy(
            src_ref=staged.at[slot, 1 - core],
            dst_ref=out_hbm.at[pl.ds(start, half)],
            send_sem=out_send_sem.at[slot],
            recv_sem=out_recv_sem.at[slot],
            device_id=sibling,
            device_id_type=MESH,
        )
        return local, remote

    done = []

    def update(at, h):
        slot = len(done)
        value = dot(p_all[at, h], mix[...]) + dot(z_all[at, h], basis_slab_t[...])
        staged[slot, 0] = value[:, :columns]
        staged[slot, 1] = value[:, columns:]
        local, remote = out_copies(slot, at, h)
        local.start()
        remote.start()
        done.append((at, h))

    update(z, 0)
    update(z, 1)
    sent = 4
    for n in range(steps):
        if sent < steps:
            image_send(sent)
            sent += 1
        for direction in range(2):
            gather_need(z_all, 2, direction, n)
            gather_need(p_all, 0, direction, n)
            update(*gather_slot(direction, n, 1))

    for slot, (at, h) in enumerate(done):
        local, remote = out_copies(slot, at, h)
        local.wait()
        remote.wait_send()
        other = pl.multiple_of((2 * at + 1 - core) * block + h * half, half)
        pltpu.make_async_remote_copy(
            src_ref=staged.at[slot, core],
            dst_ref=out_hbm.at[pl.ds(other, half)],
            send_sem=out_send_sem.at[slot],
            recv_sem=out_recv_sem.at[slot],
            device_id=sibling,
            device_id_type=MESH,
        ).wait_recv()

    for direction in range(2):
        for n in range(steps):
            gather_copy(p_all, 0, direction, n).wait_send()
            sum_copy(direction, n).wait_send()
            gather_copy(z_all, 2, direction, n).wait_send()

    @pl.loop(0, chips)
    def _(i):
        a_remote(i).wait_send()

    plane_wait_send(p_slab, 0)
    plane_wait_send(gram_recv, 1)
    plane_wait_send(gram, 2)
    plane_wait_send(z_slab, 3)
    plane_wait_send(coup_recv, 4)
    plane_wait_send(coup, 5)
    line_wait(gram_line, line_send_sem, 0)
    line_wait(coup_line, line_send_sem, 1)


def per_device(panel, image_rest, a_slab):
    f32 = jnp.float32
    rows = lax.axis_size("row")
    chips = lax.axis_size("col") // 2
    block, width = panel.shape
    columns = a_slab.shape[1]
    half = block // 2
    plane = 2 * rows
    gram_rows = width // plane
    slab = plane * PIECE
    steps = chips - 1
    dma = pltpu.SemaphoreType.DMA
    hbm = pl.BlockSpec(memory_space=pltpu.HBM)
    vmem = pl.BlockSpec(memory_space=pltpu.VMEM)
    reduction = [
        pltpu.VMEM((plane, gram_rows, width), f32),
        pltpu.VMEM((plane, gram_rows, width), f32),
        pltpu.VMEM((chips, gram_rows, width), f32),
        pltpu.VMEM((plane, gram_rows, width), f32),
    ]
    return pl.pallas_call(
        functools.partial(kernel, rows, chips),
        out_shape=(
            jax.ShapeDtypeStruct((width, width), f32),
            jax.ShapeDtypeStruct(a_slab.shape, f32),
        ),
        in_specs=[hbm, hbm, hbm],
        out_specs=(vmem, hbm),
        scratch_shapes=[
            pltpu.VMEM((2, chips, block, columns), f32),
            pltpu.VMEM((chips, 2, half, width), f32),
            pltpu.VMEM((chips, 2, half, width), f32),
            pltpu.VMEM((chips, 2, half, width), f32),
            pltpu.VMEM((2, steps, half, width), f32),
            pltpu.VMEM((2, half, width), f32),
            pltpu.VMEM((plane, PIECE, width), f32),
            pltpu.VMEM((plane, PIECE, width), f32),
            *reduction,
            *reduction,
            pltpu.VMEM((width // 2, width), f32),
            pltpu.VMEM((width, width), f32),
            pltpu.VMEM((width, slab), f32),
            pltpu.VMEM((width, slab), f32),
            pltpu.VMEM((2 * chips, 2, half, columns), f32),
            dma((4,)),
            dma((chips,)),
            dma((chips,)),
            dma((chips,)),
            dma((6,)),
            dma((6,)),
            dma((2,)),
            dma((2,)),
            dma((3, 2, steps)),
            dma((3, 2, steps)),
            dma((2 * chips,)),
            dma((2 * chips,)),
            dma((2 * chips,)),
        ],
        compiler_params=pltpu.CompilerParams(
            collective_id=0, has_side_effects=True, vmem_limit_bytes=56 * 1024 * 1024
        ),
    )(panel, image_rest, a_slab)


def solution(mesh):
    placed = (P(("row", "col"), None), P(("row", "col"), None), P("row", "col"))
    return jax.shard_map(
        per_device, mesh=mesh, in_specs=placed, out_specs=(P(), P("row", "col")), check_vma=False
    )
```

time: 824 us -> 150 us (0.18)
  waiting for transfers between devices: 658 us -> 0 us
  Pallas kernels: 0 us -> 143 us
  other arithmetic: 56.8 us -> 0 us
  matrix products: 50.4 us -> 0 us
  blocking collectives: 36.7 us -> 0 us
  between operations: 15.2 us -> 0.64 us
    psum x2 -> x0, waiting for transfers between devices: 510 us -> none  [the longest x1 256 us: per_device(): gram_matrix = lax.psum(contract_first(panel, panel), ('row', 'col'))]
    pallas_call x0 -> x1, Pallas kernels: none -> 143 us  [per_device(): pl.pallas_call(functools.partial(kernel, rows, chips), out_shape=(jax.Sha...]
    all_gather x1 -> x0, waiting for transfers between devices: 76.3 us -> none  [per_device(): lax.all_gather(paired, 'col', axis=0, tiled=True)]
    reduce_scatter x1 -> x0, waiting for transfers between devices: 71.5 us -> none  [per_device(): lax.psum_scatter(2.0 * jnp.dot(a_slab, basis_slab, precision=highest, pre...]
    another operation x9 -> x0, other arithmetic: 53.7 us -> none  [the longest x6 34 us: per_device(): lower_factor = jnp.linalg.cholesky(gram_matrix)]
    dot_general x5 -> x0, matrix products: 46.6 us -> none  [the longest x1 29.9 us: contract_last(): lax.dot_general(left, right, (((1,), (1,)), ((), ())), precision=lax.Prec...]
    all_gather x2 -> x0, blocking collectives: 36.7 us -> none  [the longest x1 18.8 us: per_device(): lax.all_gather(reduced[:slab_rows], 'row', axis=0, tiled=True)]
  transfers between devices with their start and end apart: 4 -> 0, of which waited for: 4 -> 0; matrix products, arithmetic and copies ran while one was open for 0% -> 0% of each run, Pallas kernels for 0% -> 0%
where the time goes in v1:
time: 150 us
  Pallas kernels  143 us (95%)
  local copies, waits for them, and re-layouts  6.14 us (4%)
    pallas_call x1, Pallas kernels, per_device(): pl.pallas_call(functools.partial(kernel, rows, chips), out_shape=(jax.Sha...  143 us
    unnamed x2, local copies, waits for them, and re-layouts  6.14 us

profile of v1, /device:TPU:1, one launch (start us, length us, event | category | flops | bytes accessed | tf_op | source)
XLA Modules:
  0.0 149.9 jit_solution(8522087765716206849)
XLA Ops:
  0.6 143.1 %shard_map.50 = (f32[256,256]{1,0:T(8,128)}, f32[8192,128]{1,0:T(8,128)}) custom-call(f32[512,256]{1,0:T(8,128)} %panel_hbm.1, f32[512,256]{1,0:T(8,128)} %rest_hbm.1, f32[8192,128]{1,0:T(8,128)} %a_hbm.1), custom_call_target="tpu_custom_call" | custom-call | tf_op jit(solution)/shard_map/pallas_call | solution.py:515
  143.8 1.7 %copy.7 = f32[256,256]{1,0:T(8,128)} copy(f32[256,256]{1,0:T(8,128)} %get-tuple-element.4) | data formatting | bytes 524288
  145.5 4.5 %copy.8 = f32[8192,128]{1,0:T(8,128)} copy(f32[8192,128]{1,0:T(8,128)} %get-tuple-element.5) | data formatting | bytes 8388608

commit v2 on v1

--- a/solution.py
+++ b/solution.py
@@ -25,7 +25,7 @@
     rest_hbm,
     a_hbm,
     r_ref,
-    out_hbm,
+    out_ref,
     a_buf,
     p_all,
     z_all,
@@ -34,6 +34,8 @@
     rest,
     p_slab,
     z_slab,
+    p_side,
+    z_side,
     gram_src,
     gram_recv,
     gram_line,
@@ -47,6 +49,7 @@
     basis_slab_t,
     mix,
     staged,
+    passed,
     local_sem,
     a_local_sem,
     a_send_sem,
@@ -57,9 +60,12 @@
     line_recv_sem,
     ring_send_sem,
     ring_recv_sem,
-    out_local_sem,
+    side_send_sem,
+    side_recv_sem,
     out_send_sem,
     out_recv_sem,
+    pass_send_sem,
+    pass_recv_sem,
 ):
     r = lax.axis_index("row")
     c = lax.axis_index("col")
@@ -141,6 +147,8 @@
     def _(i):
         pl.semaphore_signal(barrier, inc=1, device_id=at_chip(chip(i)), device_id_type=MESH)
 
+    for copy in panel_load:
+        copy.wait()
     pl.semaphore_wait(barrier, plane - 1 + chips - 1)
 
     def plane_copy(i, src, dst, slot):
@@ -150,6 +158,16 @@
             send_sem=plane_send_sem.at[slot],
             recv_sem=plane_recv_sem.at[slot],
             device_id=at_plane((q + i) % plane),
+            device_id_type=MESH,
+        )
+
+    def side_copy(kind, direction, src, dst):
+        return pltpu.make_async_remote_copy(
+            src_ref=src,
+            dst_ref=dst.at[q, 1 - direction],
+            send_sem=side_send_sem.at[kind, direction],
+            recv_sem=side_recv_sem.at[kind, direction],
+            device_id=(right, left)[direction],
             device_id_type=MESH,
         )
 
@@ -219,12 +237,12 @@
     waited = set()
 
     def gather_need(buf, kind, direction, n):
-        if (kind, direction, n) not in waited:
+        if n >= 0 and (kind, direction, n) not in waited:
             waited.add((kind, direction, n))
             gather_wait(buf, kind, direction, n)
 
     def gather_send(buf, kind, n):
-        if n >= steps:
+        if n >= steps - 2:
             return
         for direction in range(2):
             if n >= 2:
@@ -256,15 +274,15 @@
     def image_send(n):
         gather_send(z_all, 2, n)
 
-    for copy in panel_load:
-        copy.wait()
+    for direction in range(2):
+        side_copy(0, direction, p_all.at[z, 0, pl.ds(0, PIECE)], p_side).start()
+    panel_send(0)
     plane_gather_start(p_all.at[z, 0, pl.ds(0, PIECE)], p_slab, 0)
 
     @pl.loop(0, chips)
     def _(i):
         a_remote(i).start()
 
-    panel_send(0)
     panel_send(1)
     p_slab[q] = p_all[z, 0, 0:PIECE]
     own = p_all[z].reshape(block, width)
@@ -341,17 +359,19 @@
         scale = 1.0 / jnp.sqrt(diagonal)
         return jnp.where(col_id >= row_id, upper * scale, 0.0), work[:, nb:] * scale
 
-    sum_send(2)
+    for direction in range(2):
+        side_copy(0, direction, p_all.at[z, 0, pl.ds(0, PIECE)], p_side).wait_recv()
+    plane_gather_start(p_side.at[q], p_side, 6)
     plane_wait_recv(gram, 2)
     gram_rows = gram_src.shape[1]
     whole_gram = gram[...].reshape(plane * gram_rows, width)
     load_work(whole_gram[:nb, :nb])
     eliminate(0)
+    sum_send(2)
+    panel_send(3)
+    eliminate(chunk)
+    eliminate(2 * chunk)
     sum_send(3)
-    eliminate(chunk)
-    panel_send(3)
-    eliminate(2 * chunk)
-    sum_send(4)
     eliminate(3 * chunk)
     upper_a, inverse_a = factors()
     r_ref[:nb, :nb] = upper_a
@@ -362,23 +382,35 @@
     r_ref[nb:, :nb] = jnp.zeros((nb, nb), jnp.float32)
     lower_inv[:nb, nb:] = jnp.zeros((nb, nb), jnp.float32)
     load_work(whole_gram[nb:, nb:] - dot(cross, cross, ((0,), (0,))))
+    sum_send(4)
+    eliminate(0)
+    eliminate(chunk)
     sum_send(5)
-    eliminate(0)
-    panel_send(4)
-    eliminate(chunk)
-    sum_send(6)
     eliminate(2 * chunk)
-    panel_send(5)
     eliminate(3 * chunk)
     upper_b, inverse_b = factors()
     r_ref[nb:, nb:] = upper_b
     lower_inv[nb:, nb:] = inverse_b
     lower_inv[nb:, :nb] = -dot(inverse_b, dot(r_ref[:nb, nb:], lower_inv[:nb, :nb], ((0,), (0,))))
-
+    sum_send(6)
+    panel_send(4)
+
+    slab = plane * PIECE
     inverse = lower_inv[...]
-    basis_slab_t[...] = dot(
-        inverse, p_slab[...].reshape(plane * PIECE, width), ((1,), (1,))
-    )
+    plane_wait_recv(p_side, 6)
+
+    def columns_of(i):
+        return slice(i * slab, (i + 1) * slab)
+
+    def three(own_rows, side):
+        return (
+            own_rows[...].reshape(slab, width),
+            side[:, 0].reshape(slab, width),
+            side[:, 1].reshape(slab, width),
+        )
+
+    for i, slab_rows in enumerate(three(p_slab, p_side)):
+        basis_slab_t[:, columns_of(i)] = dot(inverse, slab_rows, ((1,), (1,)))
     own_basis = dot(p_all[z].reshape(block, width), inverse, ((1,), (1,)))
 
     for copy in rest_load:
@@ -391,92 +423,127 @@
         second = t_recv[1, steps - 2 if h == 0 else steps - 1]
         total = t_part[z, h] + first + second
         z_all[z, h] = rest[h] + 2.0 * dot(total, inverse, ((1,), (1,)))
+    for direction in range(2):
+        side_copy(1, direction, z_all.at[z, 0, pl.ds(0, PIECE)], z_side).start()
     image_send(0)
     image_send(1)
-    plane_gather_start(z_all.at[z, 0, pl.ds(0, PIECE)], z_slab, 3)
-    z_slab[q] = z_all[z, 0, 0:PIECE]
     coup_src[...] = dot(
         own_basis, z_all[z].reshape(block, width), ((0,), (0,))
     ).reshape(coup_src.shape)
     plane_scatter_start(coup_src, coup_recv, 4)
     coup_recv[q] = coup_src[q]
-    panel_send(6)
+    plane_gather_start(z_all.at[z, 0, pl.ds(0, PIECE)], z_slab, 3)
+    z_slab[q] = z_all[z, 0, 0:PIECE]
     plane_wait_recv(coup_recv, 4)
     coup_line[z] = sum_first(coup_recv, plane)
     line_start(coup_line, 1)
+    for direction in range(2):
+        side_copy(1, direction, z_all.at[z, 0, pl.ds(0, PIECE)], z_side).wait_recv()
+    plane_gather_start(z_side.at[q], z_side, 7)
     image_send(2)
     line_wait(coup_line, line_recv_sem, 1)
     coup[q] = sum_first(coup_line, chips)
     plane_gather_start(coup.at[q], coup, 5)
+    plane_wait_recv(z_slab, 3)
+    plane_wait_recv(z_side, 7)
+    plane_wait_recv(coup, 5)
     image_send(3)
-    plane_wait_recv(z_slab, 3)
-    plane_wait_recv(coup, 5)
     coupling = coup[...].reshape(width, width)
-    slab_t = basis_slab_t[...]
-    inner = jnp.transpose(z_slab[...].reshape(plane * PIECE, width))
-    inner = inner - dot(coupling, slab_t) - dot(coupling, slab_t, ((0,), (0,)))
-    mix[...] = dot(lower_inv[...], inner, ((0,), (0,)))
-
-    columns = plane * PIECE // 2
-
-    def out_copies(slot, at, h):
-        start = pl.multiple_of((2 * at + core) * block + h * half, half)
-        local = pltpu.make_async_copy(
-            staged.at[slot, core], out_hbm.at[pl.ds(start, half)], out_local_sem.at[slot]
-        )
-        remote = pltpu.make_async_remote_copy(
-            src_ref=staged.at[slot, 1 - core],
-            dst_ref=out_hbm.at[pl.ds(start, half)],
+    for i, slab_rows in enumerate(three(z_slab, z_side)):
+        slab_t = basis_slab_t[:, columns_of(i)]
+        inner = jnp.transpose(slab_rows)
+        inner = inner - dot(coupling, slab_t) - dot(coupling, slab_t, ((0,), (0,)))
+        mix[:, columns_of(i)] = dot(lower_inv[...], inner, ((0,), (0,)))
+
+    columns = slab // 2
+
+    def first_row(at, core_of_rows, h):
+        return pl.multiple_of((2 * at + core_of_rows) * block + h * half, half)
+
+    def update_block(at, h, i):
+        value = dot(p_all[at, h], mix[:, columns_of(i)])
+        value = value + dot(z_all[at, h], basis_slab_t[:, columns_of(i)])
+        return value[:, :columns], value[:, columns:]
+
+    def swap_copy(slot, start):
+        return pltpu.make_async_remote_copy(
+            src_ref=staged.at[slot],
+            dst_ref=out_ref.at[pl.ds(start, half)],
             send_sem=out_send_sem.at[slot],
             recv_sem=out_recv_sem.at[slot],
             device_id=sibling,
             device_id_type=MESH,
         )
-        return local, remote
 
     done = []
 
     def update(at, h):
         slot = len(done)
-        value = dot(p_all[at, h], mix[...]) + dot(z_all[at, h], basis_slab_t[...])
-        staged[slot, 0] = value[:, :columns]
-        staged[slot, 1] = value[:, columns:]
-        local, remote = out_copies(slot, at, h)
-        local.start()
-        remote.start()
+        low, high = update_block(at, h, 0)
+        staged[slot] = jnp.where(core == 0, high, low)
+        start = first_row(at, core, h)
+        swap_copy(slot, start).start()
+        out_ref[pl.ds(start, half), :] = jnp.where(core == 0, low, high)
         done.append((at, h))
 
-    update(z, 0)
-    update(z, 1)
-    sent = 4
-    for n in range(steps):
-        if sent < steps:
-            image_send(sent)
-            sent += 1
+    def pass_copy(direction, n, source, target, at, h):
+        return pltpu.make_async_remote_copy(
+            src_ref=passed.at[direction, n, target],
+            dst_ref=out_ref.at[pl.ds(first_row(at, source, h), half)],
+            send_sem=pass_send_sem.at[direction, n, target],
+            recv_sem=pass_recv_sem.at[direction, n, source],
+            device_id=(r, 2 * chip(1 if direction == 0 else -1) + target),
+            device_id_type=MESH,
+        )
+
+    def pass_send(n):
+        for direction in range(2):
+            last = steps - 2 + n
+            gather_need(z_all, 2, direction, last - 2)
+            gather_need(p_all, 0, direction, last - 2)
+            at, h = gather_slot(direction, last, 0)
+            low, high = update_block(at, h, 1 + direction)
+            passed[direction, n, 0] = low
+            passed[direction, n, 1] = high
+            for target in range(2):
+                pass_copy(direction, n, core, target, at, h).start()
+
+    def update_received(n):
         for direction in range(2):
             gather_need(z_all, 2, direction, n)
             gather_need(p_all, 0, direction, n)
             update(*gather_slot(direction, n, 1))
 
+    image_send(4)
+    update(z, 0)
+    update(z, 1)
+    for n in range(steps - 4):
+        update_received(n)
+    pass_send(0)
+    pass_send(1)
+    for n in range(max(steps - 4, 0), steps - 2):
+        update_received(n)
+
     for slot, (at, h) in enumerate(done):
-        local, remote = out_copies(slot, at, h)
-        local.wait()
-        remote.wait_send()
-        other = pl.multiple_of((2 * at + 1 - core) * block + h * half, half)
-        pltpu.make_async_remote_copy(
-            src_ref=staged.at[slot, core],
-            dst_ref=out_hbm.at[pl.ds(other, half)],
-            send_sem=out_send_sem.at[slot],
-            recv_sem=out_recv_sem.at[slot],
-            device_id=sibling,
-            device_id_type=MESH,
-        ).wait_recv()
+        swap_copy(slot, first_row(at, core, h)).wait_send()
+        swap_copy(slot, first_row(at, 1 - core, h)).wait_recv()
+    for n in range(2):
+        for direction in range(2):
+            last = steps - 2 + n
+            for index in range(2):
+                at, h = gather_slot(direction, last, 0)
+                pass_copy(direction, n, core, index, at, h).wait_send()
+                at, h = gather_slot(direction, last, 1)
+                pass_copy(direction, n, index, index, at, h).wait_recv()
 
     for direction in range(2):
         for n in range(steps):
+            sum_copy(direction, n).wait_send()
+        for n in range(steps - 2):
             gather_copy(p_all, 0, direction, n).wait_send()
-            sum_copy(direction, n).wait_send()
             gather_copy(z_all, 2, direction, n).wait_send()
+        side_copy(0, direction, p_all.at[z, 0, pl.ds(0, PIECE)], p_side).wait_send()
+        side_copy(1, direction, z_all.at[z, 0, pl.ds(0, PIECE)], z_side).wait_send()
 
     @pl.loop(0, chips)
     def _(i):
@@ -488,6 +555,8 @@
     plane_wait_send(z_slab, 3)
     plane_wait_send(coup_recv, 4)
     plane_wait_send(coup, 5)
+    plane_wait_send(p_side, 6)
+    plane_wait_send(z_side, 7)
     line_wait(gram_line, line_send_sem, 0)
     line_wait(coup_line, line_send_sem, 1)
 
@@ -515,11 +584,11 @@
     return pl.pallas_call(
         functools.partial(kernel, rows, chips),
         out_shape=(
-            jax.ShapeDtypeStruct((width, width), f32),
-            jax.ShapeDtypeStruct(a_slab.shape, f32),
+            pltpu.VMEM((width, width), f32),
+            pltpu.VMEM(a_slab.shape, f32),
         ),
         in_specs=[hbm, hbm, hbm],
-        out_specs=(vmem, hbm),
+        out_specs=(vmem, vmem),
         scratch_shapes=[
             pltpu.VMEM((2, chips, block, columns), f32),
             pltpu.VMEM((chips, 2, half, width), f32),
@@ -529,26 +598,32 @@
             pltpu.VMEM((2, half, width), f32),
             pltpu.VMEM((plane, PIECE, width), f32),
             pltpu.VMEM((plane, PIECE, width), f32),
+            pltpu.VMEM((plane, 2, PIECE, width), f32),
+            pltpu.VMEM((plane, 2, PIECE, width), f32),
             *reduction,
             *reduction,
             pltpu.VMEM((width // 2, width), f32),
             pltpu.VMEM((width, width), f32),
-            pltpu.VMEM((width, slab), f32),
-            pltpu.VMEM((width, slab), f32),
-            pltpu.VMEM((2 * chips, 2, half, columns), f32),
+            pltpu.VMEM((width, 3 * slab), f32),
+            pltpu.VMEM((width, 3 * slab), f32),
+            pltpu.VMEM((2 * chips - 4, half, columns), f32),
+            pltpu.VMEM((2, 2, 2, half, columns), f32),
             dma((4,)),
             dma((chips,)),
             dma((chips,)),
             dma((chips,)),
-            dma((6,)),
-            dma((6,)),
+            dma((8,)),
+            dma((8,)),
             dma((2,)),
             dma((2,)),
             dma((3, 2, steps)),
             dma((3, 2, steps)),
-            dma((2 * chips,)),
-            dma((2 * chips,)),
-            dma((2 * chips,)),
+            dma((2, 2)),
+            dma((2, 2)),
+            dma((2 * chips - 4,)),
+            dma((2 * chips - 4,)),
+            dma((2, 2, 2)),
+            dma((2, 2, 2)),
         ],
         compiler_params=pltpu.CompilerParams(
             collective_id=0, has_side_effects=True, vmem_limit_bytes=56 * 1024 * 1024

time: 150 us -> 142 us (0.947)
  Pallas kernels: 143 us -> 138 us
  local copies, waits for them, and re-layouts: 6.14 us -> 2.72 us
    pallas_call x1, Pallas kernels: 143 us -> 138 us  [per_device(): pl.pallas_call(functools.partial(kernel, rows, chips), out_shape=(pltpu.V...]
    unnamed x2, local copies, waits for them, and re-layouts: 6.14 us -> 2.72 us
where the time goes in v2:
time: 142 us
  Pallas kernels  138 us (97%)
  local copies, waits for them, and re-layouts  2.72 us (2%)
    pallas_call x1, Pallas kernels, per_device(): pl.pallas_call(functools.partial(kernel, rows, chips), out_shape=(pltpu.V...  138 us

profile of v2, /device:TPU:1, one launch (start us, length us, event | category | flops | bytes accessed | tf_op | source)
XLA Modules:
  0.0 141.7 jit_solution(10338433703749993804)
XLA Ops:
  0.6 138.3 %shard_map.50 = (f32[256,256]{1,0:T(8,128)S(1)}, f32[8192,128]{1,0:T(8,128)S(1)}) custom-call(f32[512,256]{1,0:T(8,128)} %panel_hbm.1, f32[512,256]{1,0:T(8,128)} %rest_hbm.1, f32[8192,128]{1,0:T(8,128)} %a_hbm.1), custom_call_target="tpu_custom_call" | custom-call | tf_op jit(solution)/shard_map/pallas_call | solution.py:584
  139.0 0.7 copy.7
  139.7 2.0 %copy.8 = f32[8192,128]{1,0:T(8,128)} copy(f32[8192,128]{1,0:T(8,128)S(1)} %get-tuple-element.3) | data formatting | bytes 8388608

commit v3 on v2

--- a/solution.py
+++ b/solution.py
@@ -277,18 +277,17 @@
     for direction in range(2):
         side_copy(0, direction, p_all.at[z, 0, pl.ds(0, PIECE)], p_side).start()
     panel_send(0)
-    plane_gather_start(p_all.at[z, 0, pl.ds(0, PIECE)], p_slab, 0)
 
     @pl.loop(0, chips)
     def _(i):
         a_remote(i).start()
 
-    panel_send(1)
-    p_slab[q] = p_all[z, 0, 0:PIECE]
     own = p_all[z].reshape(block, width)
     gram_src[...] = dot(own, own, ((0,), (0,))).reshape(gram_src.shape)
     plane_scatter_start(gram_src, gram_recv, 1)
     gram_recv[q] = gram_src[q]
+    plane_gather_start(p_all.at[z, 0, pl.ds(0, PIECE)], p_slab, 0)
+    p_slab[q] = p_all[z, 0, 0:PIECE]
 
     def partial_sums(i):
         target = block_of(i)
@@ -305,6 +304,10 @@
         both = jnp.concatenate([a_buf[0, target], a_buf[1, target]], axis=1)
         t_part[target] = dot(both, slab).reshape(2, half, width)
 
+    plane_wait_recv(gram_recv, 1)
+    gram_line[z] = sum_first(gram_recv, plane)
+    line_start(gram_line, 0)
+    panel_send(1)
     plane_wait_recv(p_slab, 0)
     partial_sums(0)
     sum_send(0)
@@ -314,18 +317,14 @@
         partial_sums(i)
 
     sum_send(1)
-
-    @pl.loop(3, chips)
-    def _(i):
-        partial_sums(i)
-
-    plane_wait_recv(gram_recv, 1)
-    gram_line[z] = sum_first(gram_recv, plane)
-    line_start(gram_line, 0)
     panel_send(2)
     line_wait(gram_line, line_recv_sem, 0)
     gram[q] = sum_first(gram_line, chips)
     plane_gather_start(gram.at[q], gram, 2)
+
+    @pl.loop(3, chips)
+    def _(i):
+        partial_sums(i)
 
     nb = width // 2
     chunk = nb // 4
@@ -367,9 +366,8 @@
     whole_gram = gram[...].reshape(plane * gram_rows, width)
     load_work(whole_gram[:nb, :nb])
     eliminate(0)
+    eliminate(chunk)
     sum_send(2)
-    panel_send(3)
-    eliminate(chunk)
     eliminate(2 * chunk)
     sum_send(3)
     eliminate(3 * chunk)
@@ -382,18 +380,19 @@
     r_ref[nb:, :nb] = jnp.zeros((nb, nb), jnp.float32)
     lower_inv[:nb, nb:] = jnp.zeros((nb, nb), jnp.float32)
     load_work(whole_gram[nb:, nb:] - dot(cross, cross, ((0,), (0,))))
+    eliminate(0)
     sum_send(4)
-    eliminate(0)
     eliminate(chunk)
     sum_send(5)
     eliminate(2 * chunk)
+    sum_send(6)
+    panel_send(3)
+    panel_send(4)
     eliminate(3 * chunk)
     upper_b, inverse_b = factors()
     r_ref[nb:, nb:] = upper_b
     lower_inv[nb:, nb:] = inverse_b
     lower_inv[nb:, :nb] = -dot(inverse_b, dot(r_ref[:nb, nb:], lower_inv[:nb, :nb], ((0,), (0,))))
-    sum_send(6)
-    panel_send(4)
 
     slab = plane * PIECE
     inverse = lower_inv[...]
@@ -426,7 +425,6 @@
     for direction in range(2):
         side_copy(1, direction, z_all.at[z, 0, pl.ds(0, PIECE)], z_side).start()
     image_send(0)
-    image_send(1)
     coup_src[...] = dot(
         own_basis, z_all[z].reshape(block, width), ((0,), (0,))
     ).reshape(coup_src.shape)
@@ -437,6 +435,7 @@
     plane_wait_recv(coup_recv, 4)
     coup_line[z] = sum_first(coup_recv, plane)
     line_start(coup_line, 1)
+    image_send(1)
     for direction in range(2):
         side_copy(1, direction, z_all.at[z, 0, pl.ds(0, PIECE)], z_side).wait_recv()
     plane_gather_start(z_side.at[q], z_side, 7)
@@ -444,10 +443,10 @@
     line_wait(coup_line, line_recv_sem, 1)
     coup[q] = sum_first(coup_line, chips)
     plane_gather_start(coup.at[q], coup, 5)
+    image_send(3)
     plane_wait_recv(z_slab, 3)
     plane_wait_recv(z_side, 7)
     plane_wait_recv(coup, 5)
-    image_send(3)
     coupling = coup[...].reshape(width, width)
     for i, slab_rows in enumerate(three(z_slab, z_side)):
         slab_t = basis_slab_t[:, columns_of(i)]
@@ -514,10 +513,11 @@
             gather_need(p_all, 0, direction, n)
             update(*gather_slot(direction, n, 1))
 
-    image_send(4)
     update(z, 0)
     update(z, 1)
     for n in range(steps - 4):
+        if n == 1:
+            image_send(4)
         update_received(n)
     pass_send(0)
     pass_send(1)

time: 142 us -> 130 us (0.915)
  Pallas kernels: 138 us -> 127 us
    pallas_call x1, Pallas kernels: 138 us -> 127 us  [per_device(): pl.pallas_call(functools.partial(kernel, rows, chips), out_shape=(pltpu.V...]
where the time goes in v3:
time: 130 us
  Pallas kernels  127 us (98%)
  local copies, waits for them, and re-layouts  2.72 us (2%)
    pallas_call x1, Pallas kernels, per_device(): pl.pallas_call(functools.partial(kernel, rows, chips), out_shape=(pltpu.V...  127 us
    unnamed x2, local copies, waits for them, and re-layouts  2.72 us

profile of v3, /device:TPU:1, one launch (start us, length us, event | category | flops | bytes accessed | tf_op | source)
XLA Modules:
  0.0 130.0 jit_solution(14231122782629559542)
XLA Ops:
  0.6 126.7 %shard_map.50 = (f32[256,256]{1,0:T(8,128)S(1)}, f32[8192,128]{1,0:T(8,128)S(1)}) custom-call(f32[512,256]{1,0:T(8,128)} %panel_hbm.1, f32[512,256]{1,0:T(8,128)} %rest_hbm.1, f32[8192,128]{1,0:T(8,128)} %a_hbm.1), custom_call_target="tpu_custom_call" | custom-call | tf_op jit(solution)/shard_map/pallas_call | solution.py:584
  127.3 0.7 copy.7
  128.0 2.0 %copy.8 = f32[8192,128]{1,0:T(8,128)} copy(f32[8192,128]{1,0:T(8,128)S(1)} %get-tuple-element.3) | data formatting | bytes 8388608

commit v4 on v3

--- a/solution.py
+++ b/solution.py
@@ -42,7 +42,7 @@
     gram,
     coup_src,
     coup_recv,
-    coup_line,
+    coup_piece,
     coup,
     work,
     lower_inv,
@@ -128,12 +128,8 @@
             device_id_type=MESH,
         )
 
-    for copy in panel_load + rest_load:
+    for copy in panel_load:
         copy.start()
-
-    @pl.loop(0, chips)
-    def _(i):
-        a_local(i).start()
 
     barrier = pltpu.get_barrier_semaphore()
 
@@ -146,6 +142,13 @@
     @pl.loop(1, chips)
     def _(i):
         pl.semaphore_signal(barrier, inc=1, device_id=at_chip(chip(i)), device_id_type=MESH)
+
+    for copy in rest_load:
+        copy.start()
+
+    @pl.loop(0, chips)
+    def _(i):
+        a_local(i).start()
 
     for copy in panel_load:
         copy.wait()
@@ -189,17 +192,40 @@
         whole = dst.at[pl.ds(0, plane - 1)]
         pltpu.make_async_copy(whole, whole, plane_send_sem.at[slot]).wait()
 
-    def line_start(buf, slot):
+    def line_copy(i, src, dst, slot):
+        return pltpu.make_async_remote_copy(
+            src_ref=src,
+            dst_ref=dst,
+            send_sem=line_send_sem.at[slot],
+            recv_sem=line_recv_sem.at[slot],
+            device_id=at_chip(chip(i)),
+            device_id_type=MESH,
+        )
+
+    def line_scatter(total, src, dst, slot):
+        share = src.shape[1]
+        for i in range(chips):
+            src[i] = total[i * share : (i + 1) * share]
+
         @pl.loop(1, chips)
         def _(i):
-            pltpu.make_async_remote_copy(
-                src_ref=buf.at[z],
-                dst_ref=buf.at[z],
-                send_sem=line_send_sem.at[slot],
-                recv_sem=line_recv_sem.at[slot],
-                device_id=at_chip(chip(i)),
-                device_id_type=MESH,
-            ).start()
+            line_copy(i, src.at[chip(i)], dst.at[z], slot).start()
+
+        dst[z] = src[z]
+
+    def line_gather(received, dst, slot):
+        line_wait(received, line_recv_sem, slot)
+        dst[z] = sum_first(received, chips)
+
+        @pl.loop(1, chips)
+        def _(i):
+            line_copy(i, dst.at[z], dst.at[z], slot + 1).start()
+
+    def line_finish(gathered, dst, slot):
+        line_wait(gathered, line_recv_sem, slot + 1)
+        share = gathered.shape[1]
+        for i in range(chips):
+            dst[q, i * share : (i + 1) * share] = gathered[i]
 
     def line_wait(buf, sem, slot):
         whole = buf.at[pl.ds(0, chips - 1)]
@@ -305,11 +331,11 @@
         t_part[target] = dot(both, slab).reshape(2, half, width)
 
     plane_wait_recv(gram_recv, 1)
-    gram_line[z] = sum_first(gram_recv, plane)
-    line_start(gram_line, 0)
+    line_scatter(sum_first(gram_recv, plane), gram_line.at[0], gram_line.at[1], 0)
     panel_send(1)
     plane_wait_recv(p_slab, 0)
     partial_sums(0)
+    line_gather(gram_line.at[1], gram_line.at[2], 0)
     sum_send(0)
 
     @pl.loop(1, 3)
@@ -318,8 +344,7 @@
 
     sum_send(1)
     panel_send(2)
-    line_wait(gram_line, line_recv_sem, 0)
-    gram[q] = sum_first(gram_line, chips)
+    line_finish(gram_line.at[2], gram, 0)
     plane_gather_start(gram.at[q], gram, 2)
 
     @pl.loop(3, chips)
@@ -433,15 +458,19 @@
     plane_gather_start(z_all.at[z, 0, pl.ds(0, PIECE)], z_slab, 3)
     z_slab[q] = z_all[z, 0, 0:PIECE]
     plane_wait_recv(coup_recv, 4)
-    coup_line[z] = sum_first(coup_recv, plane)
-    line_start(coup_line, 1)
+    coup_piece[z] = sum_first(coup_recv, plane)
+
+    @pl.loop(1, chips)
+    def _(i):
+        line_copy(i, coup_piece.at[z], coup_piece.at[z], 2).start()
+
     image_send(1)
     for direction in range(2):
         side_copy(1, direction, z_all.at[z, 0, pl.ds(0, PIECE)], z_side).wait_recv()
     plane_gather_start(z_side.at[q], z_side, 7)
     image_send(2)
-    line_wait(coup_line, line_recv_sem, 1)
-    coup[q] = sum_first(coup_line, chips)
+    line_wait(coup_piece, line_recv_sem, 2)
+    coup[q] = sum_first(coup_piece, chips)
     plane_gather_start(coup.at[q], coup, 5)
     image_send(3)
     plane_wait_recv(z_slab, 3)
@@ -515,14 +544,39 @@
 
     update(z, 0)
     update(z, 1)
-    for n in range(steps - 4):
-        if n == 1:
-            image_send(4)
+    update_received(0)
+    image_send(4)
+    pass_send(0)
+    if steps > 4:
+        update_received(1)
+    pass_send(1)
+    for n in range(2, steps - 2):
         update_received(n)
-    pass_send(0)
-    pass_send(1)
-    for n in range(max(steps - 4, 0), steps - 2):
-        update_received(n)
+
+    for direction in range(2):
+        for n in range(steps):
+            sum_copy(direction, n).wait_send()
+        for n in range(steps - 2):
+            gather_copy(p_all, 0, direction, n).wait_send()
+            gather_copy(z_all, 2, direction, n).wait_send()
+        side_copy(0, direction, p_all.at[z, 0, pl.ds(0, PIECE)], p_side).wait_send()
+        side_copy(1, direction, z_all.at[z, 0, pl.ds(0, PIECE)], z_side).wait_send()
+
+    @pl.loop(0, chips)
+    def _(i):
+        a_remote(i).wait_send()
+
+    plane_wait_send(p_slab, 0)
+    plane_wait_send(gram_recv, 1)
+    plane_wait_send(gram, 2)
+    plane_wait_send(z_slab, 3)
+    plane_wait_send(coup_recv, 4)
+    plane_wait_send(coup, 5)
+    plane_wait_send(p_side, 6)
+    plane_wait_send(z_side, 7)
+    for slot in range(2):
+        line_wait(gram_line.at[1], line_send_sem, slot)
+    line_wait(coup_piece, line_send_sem, 2)
 
     for slot, (at, h) in enumerate(done):
         swap_copy(slot, first_row(at, core, h)).wait_send()
@@ -535,30 +589,6 @@
                 pass_copy(direction, n, core, index, at, h).wait_send()
                 at, h = gather_slot(direction, last, 1)
                 pass_copy(direction, n, index, index, at, h).wait_recv()
-
-    for direction in range(2):
-        for n in range(steps):
-            sum_copy(direction, n).wait_send()
-        for n in range(steps - 2):
-            gather_copy(p_all, 0, direction, n).wait_send()
-            gather_copy(z_all, 2, direction, n).wait_send()
-        side_copy(0, direction, p_all.at[z, 0, pl.ds(0, PIECE)], p_side).wait_send()
-        side_copy(1, direction, z_all.at[z, 0, pl.ds(0, PIECE)], z_side).wait_send()
-
-    @pl.loop(0, chips)
-    def _(i):
-        a_remote(i).wait_send()
-
-    plane_wait_send(p_slab, 0)
-    plane_wait_send(gram_recv, 1)
-    plane_wait_send(gram, 2)
-    plane_wait_send(z_slab, 3)
-    plane_wait_send(coup_recv, 4)
-    plane_wait_send(coup, 5)
-    plane_wait_send(p_side, 6)
-    plane_wait_send(z_side, 7)
-    line_wait(gram_line, line_send_sem, 0)
-    line_wait(coup_line, line_send_sem, 1)
 
 
 def per_device(panel, image_rest, a_slab):
@@ -575,12 +605,9 @@
     dma = pltpu.SemaphoreType.DMA
     hbm = pl.BlockSpec(memory_space=pltpu.HBM)
     vmem = pl.BlockSpec(memory_space=pltpu.VMEM)
-    reduction = [
-        pltpu.VMEM((plane, gram_rows, width), f32),
-        pltpu.VMEM((plane, gram_rows, width), f32),
-        pltpu.VMEM((chips, gram_rows, width), f32),
-        pltpu.VMEM((plane, gram_rows, width), f32),
-    ]
+    piece = pltpu.VMEM((plane, gram_rows, width), f32)
+    gram_line = pltpu.VMEM((3, chips, gram_rows // chips, width), f32)
+    coup_piece = pltpu.VMEM((chips, gram_rows, width), f32)
     return pl.pallas_call(
         functools.partial(kernel, rows, chips),
         out_shape=(
@@ -600,8 +627,14 @@
             pltpu.VMEM((plane, PIECE, width), f32),
             pltpu.VMEM((plane, 2, PIECE, width), f32),
             pltpu.VMEM((plane, 2, PIECE, width), f32),
-            *reduction,
-            *reduction,
+            piece,
+            piece,
+            gram_line,
+            piece,
+            piece,
+            piece,
+            coup_piece,
+            piece,
             pltpu.VMEM((width // 2, width), f32),
             pltpu.VMEM((width, width), f32),
             pltpu.VMEM((width, 3 * slab), f32),
@@ -614,8 +647,8 @@
             dma((chips,)),
             dma((8,)),
             dma((8,)),
-            dma((2,)),
-            dma((2,)),
+            dma((4,)),
+            dma((4,)),
             dma((3, 2, steps)),
             dma((3, 2, steps)),
             dma((2, 2)),

time: 130 us -> 129 us (level)
  no operation moved by 1% of the time
where the time goes in v4:
time: 129 us
  Pallas kernels  126 us (98%)
  local copies, waits for them, and re-layouts  2.72 us (2%)
    pallas_call x1, Pallas kernels, per_device(): pl.pallas_call(functools.partial(kernel, rows, chips), out_shape=(pltpu.V...  126 us
    unnamed x2, local copies, waits for them, and re-layouts  2.72 us

profile of v4, /device:TPU:1, one launch (start us, length us, event | category | flops | bytes accessed | tf_op | source)
XLA Modules:
  0.0 129.1 jit_solution(7187098860773111699)
XLA Ops:
  0.6 125.8 %shard_map.50 = (f32[256,256]{1,0:T(8,128)S(1)}, f32[8192,128]{1,0:T(8,128)S(1)}) custom-call(f32[512,256]{1,0:T(8,128)} %panel_hbm.1, f32[512,256]{1,0:T(8,128)} %rest_hbm.1, f32[8192,128]{1,0:T(8,128)} %a_hbm.1), custom_call_target="tpu_custom_call" | custom-call | tf_op jit(solution)/shard_map/pallas_call | solution.py:611
  126.4 0.7 copy.7
  127.1 2.0 %copy.8 = f32[8192,128]{1,0:T(8,128)} copy(f32[8192,128]{1,0:T(8,128)S(1)} %get-tuple-element.3) | data formatting | bytes 8388608

commit v5 on v4

--- a/solution.py
+++ b/solution.py
@@ -300,6 +300,13 @@
     def image_send(n):
         gather_send(z_all, 2, n)
 
+    def panel_send_part(part):
+        share = half // 2
+        for direction in range(2):
+            at, h = gather_slot(direction, 1, 0)
+            place = p_all.at[at, h, pl.ds(part * share, share)]
+            ring(0, direction, 1, place, place).start()
+
     for direction in range(2):
         side_copy(0, direction, p_all.at[z, 0, pl.ds(0, PIECE)], p_side).start()
     panel_send(0)
@@ -330,9 +337,10 @@
         both = jnp.concatenate([a_buf[0, target], a_buf[1, target]], axis=1)
         t_part[target] = dot(both, slab).reshape(2, half, width)
 
+    panel_send_part(0)
     plane_wait_recv(gram_recv, 1)
     line_scatter(sum_first(gram_recv, plane), gram_line.at[0], gram_line.at[1], 0)
-    panel_send(1)
+    panel_send_part(1)
     plane_wait_recv(p_slab, 0)
     partial_sums(0)
     line_gather(gram_line.at[1], gram_line.at[2], 0)
@@ -383,6 +391,7 @@
         scale = 1.0 / jnp.sqrt(diagonal)
         return jnp.where(col_id >= row_id, upper * scale, 0.0), work[:, nb:] * scale
 
+    sum_send(2)
     for direction in range(2):
         side_copy(0, direction, p_all.at[z, 0, pl.ds(0, PIECE)], p_side).wait_recv()
     plane_gather_start(p_side.at[q], p_side, 6)
@@ -392,10 +401,10 @@
     load_work(whole_gram[:nb, :nb])
     eliminate(0)
     eliminate(chunk)
-    sum_send(2)
+    sum_send(3)
     eliminate(2 * chunk)
-    sum_send(3)
     eliminate(3 * chunk)
+    sum_send(4)
     upper_a, inverse_a = factors()
     r_ref[:nb, :nb] = upper_a
     lower_inv[:nb, :nb] = inverse_a
@@ -406,11 +415,10 @@
     lower_inv[:nb, nb:] = jnp.zeros((nb, nb), jnp.float32)
     load_work(whole_gram[nb:, nb:] - dot(cross, cross, ((0,), (0,))))
     eliminate(0)
-    sum_send(4)
+    sum_send(5)
     eliminate(chunk)
-    sum_send(5)
+    sum_send(6)
     eliminate(2 * chunk)
-    sum_send(6)
     panel_send(3)
     panel_send(4)
     eliminate(3 * chunk)

time: 129 us -> 128 us (level)
  Pallas kernels: 126 us -> 124 us
    pallas_call x1, Pallas kernels: 126 us -> 124 us  [per_device(): pl.pallas_call(functools.partial(kernel, rows, chips), out_shape=(pltpu.V...]
where the time goes in v5:
time: 128 us; the launch traced here: 127 us
  Pallas kernels  124 us (97%)
  local copies, waits for them, and re-layouts  2.72 us (2%)
    pallas_call x1, Pallas kernels, per_device(): pl.pallas_call(functools.partial(kernel, rows, chips), out_shape=(pltpu.V...  124 us
    unnamed x2, local copies, waits for them, and re-layouts  2.72 us

profile of v5, /device:TPU:1, one launch (start us, length us, event | category | flops | bytes accessed | tf_op | source)
XLA Modules:
  0.0 127.4 jit_solution(16927157862368767317)
XLA Ops:
  0.6 124.1 %shard_map.50 = (f32[256,256]{1,0:T(8,128)S(1)}, f32[8192,128]{1,0:T(8,128)S(1)}) custom-call(f32[512,256]{1,0:T(8,128)} %panel_hbm.1, f32[512,256]{1,0:T(8,128)} %rest_hbm.1, f32[8192,128]{1,0:T(8,128)} %a_hbm.1), custom_call_target="tpu_custom_call" | custom-call | tf_op jit(solution)/shard_map/pallas_call | solution.py:619
  124.7 0.7 copy.7
  125.4 2.0 %copy.8 = f32[8192,128]{1,0:T(8,128)} copy(f32[8192,128]{1,0:T(8,128)S(1)} %get-tuple-element.3) | data formatting | bytes 8388608

commit v6 on v5

--- a/solution.py
+++ b/solution.py
@@ -42,7 +42,7 @@
     gram,
     coup_src,
     coup_recv,
-    coup_piece,
+    coup_line,
     coup,
     work,
     lower_inv,
@@ -420,7 +420,6 @@
     sum_send(6)
     eliminate(2 * chunk)
     panel_send(3)
-    panel_send(4)
     eliminate(3 * chunk)
     upper_b, inverse_b = factors()
     r_ref[nb:, nb:] = upper_b
@@ -466,19 +465,15 @@
     plane_gather_start(z_all.at[z, 0, pl.ds(0, PIECE)], z_slab, 3)
     z_slab[q] = z_all[z, 0, 0:PIECE]
     plane_wait_recv(coup_recv, 4)
-    coup_piece[z] = sum_first(coup_recv, plane)
-
-    @pl.loop(1, chips)
-    def _(i):
-        line_copy(i, coup_piece.at[z], coup_piece.at[z], 2).start()
-
+    line_scatter(sum_first(coup_recv, plane), coup_line.at[0], coup_line.at[1], 2)
     image_send(1)
     for direction in range(2):
         side_copy(1, direction, z_all.at[z, 0, pl.ds(0, PIECE)], z_side).wait_recv()
     plane_gather_start(z_side.at[q], z_side, 7)
+    line_gather(coup_line.at[1], coup_line.at[2], 2)
+    panel_send(4)
     image_send(2)
-    line_wait(coup_piece, line_recv_sem, 2)
-    coup[q] = sum_first(coup_piece, chips)
+    line_finish(coup_line.at[2], coup, 2)
     plane_gather_start(coup.at[q], coup, 5)
     image_send(3)
     plane_wait_recv(z_slab, 3)
@@ -584,7 +579,7 @@
     plane_wait_send(z_side, 7)
     for slot in range(2):
         line_wait(gram_line.at[1], line_send_sem, slot)
-    line_wait(coup_piece, line_send_sem, 2)
+        line_wait(coup_line.at[1], line_send_sem, 2 + slot)
 
     for slot, (at, h) in enumerate(done):
         swap_copy(slot, first_row(at, core, h)).wait_send()
@@ -615,7 +610,6 @@
     vmem = pl.BlockSpec(memory_space=pltpu.VMEM)
     piece = pltpu.VMEM((plane, gram_rows, width), f32)
     gram_line = pltpu.VMEM((3, chips, gram_rows // chips, width), f32)
-    coup_piece = pltpu.VMEM((chips, gram_rows, width), f32)
     return pl.pallas_call(
         functools.partial(kernel, rows, chips),
         out_shape=(
@@ -641,7 +635,7 @@
             piece,
             piece,
             piece,
-            coup_piece,
+            gram_line,
             piece,
             pltpu.VMEM((width // 2, width), f32),
             pltpu.VMEM((width, width), f32),

time: 128 us -> 127 us (level)
  no operation moved by 1% of the time
where the time goes in v6:
time: 127 us; the launch traced here: 126 us
  Pallas kernels  123 us (97%)
  local copies, waits for them, and re-layouts  2.72 us (2%)
    pallas_call x1, Pallas kernels, per_device(): pl.pallas_call(functools.partial(kernel, rows, chips), out_shape=(pltpu.V...  123 us
    unnamed x2, local copies, waits for them, and re-layouts  2.72 us

profile of v6, /device:TPU:1, one launch (start us, length us, event | category | flops | bytes accessed | tf_op | source)
XLA Modules:
  0.0 126.4 jit_solution(10534783342745827583)
XLA Ops:
  0.6 123.1 %shard_map.50 = (f32[256,256]{1,0:T(8,128)S(1)}, f32[8192,128]{1,0:T(8,128)S(1)}) custom-call(f32[512,256]{1,0:T(8,128)} %panel_hbm.1, f32[512,256]{1,0:T(8,128)} %rest_hbm.1, f32[8192,128]{1,0:T(8,128)} %a_hbm.1), custom_call_target="tpu_custom_call" | custom-call | tf_op jit(solution)/shard_map/pallas_call | solution.py:613
  123.7 0.7 copy.7
  124.4 2.0 %copy.8 = f32[8192,128]{1,0:T(8,128)} copy(f32[8192,128]{1,0:T(8,128)S(1)} %get-tuple-element.3) | data formatting | bytes 8388608
